TPU v7x, 256 devices: a whole 4x4x8 slice. The times are simulated.
256 devices in a mesh: section: 2 (over y_lo), fsdp: 32 (over x, z), dp: 4 (over y_hi, core).
Axes of the slice: x: 4, y: 4 (y_hi: 2, y_lo: 2; y = y_hi * 2 + y_lo), z: 8, core: 2. Of those that a mesh axis runs over, the one named last changes fastest.
Arguments:
- activations: bfloat16 [2, 4, 4096, 3584], P('section', None, ('fsdp', 'dp')), may hold values from -6 to 6
- out_grad: bfloat16 [2, 4, 4096, 14336], P('section', None, ('fsdp', 'dp')), may hold values from -6 to 6
- blocks: bfloat16 [2, 128, 128, 128], P('section', 'fsdp'), may hold values from -0.5 to 0.5
- pattern: int32 [2, 128, 2], P('section', 'fsdp'), may hold values from 0 to 111, as said below
- order: int32 [4], replicated, may hold values from 0 to 3, each once
Outputs:
- received: bfloat16 [2, 4, 4096, 3584], P('section', None, ('fsdp', 'dp'))
- weight_grad: float32 [2, 128, 128, 128], P('section', 'fsdp')
Inputs may be any that keep to these rules, and one draw needn't show every extreme that they name: pattern[s, b, 0] < 28 and pattern[s, b, 1] < 112; no two blocks of one section share both indices; within a section the blocks stand in ascending order of (row, column). `order`: a permutation of the microbatches.
All inputs are finite; a program needn't handle non-finite values.
Results may differ from a plain program's by a relative error of at most 0.0049.
Values may be sent and summed in bfloat16 or wider, within the bound.
A program may use at most 128 MiB of HBM per device.

v0:
```python
import math
import jax
import jax.numpy as jnp
from jax import lax
from jax.sharding import PartitionSpec as P


def passed_along(block, axis, distance):
    devices = range(lax.axis_size(axis))
    route = [(i - distance, i) for i in devices if i - distance in devices]
    return lax.ppermute(block, axis, route)


def silu_slope(pre_act):
    sigmoid_val = jax.nn.sigmoid(pre_act)
    return sigmoid_val * (1.0 + pre_act * (1.0 - sigmoid_val))


def in_groups(step_fn, running, shard_blocks):
    block_count = shard_blocks.shape[0]
    group_size = math.gcd(block_count, 32)

    def one_group(number, carried):
        segment = lax.dynamic_slice_in_dim(shard_blocks, number * group_size, group_size, 0)
        return step_fn(carried, segment, number * group_size)

    return lax.fori_loop(0, block_count // group_size, one_group, running)


def local(activations, out_grad, blocks, pattern, order):
    block_size = blocks.shape[-1]
    micro_count = activations.shape[1]
    tok_rows = activations.shape[1] * activations.shape[2]
    row_count = activations.shape[3] // block_size
    col_count = out_grad.shape[3] // block_size
    features = activations[0].reshape(tok_rows, row_count, block_size)
    hidden_grad = out_grad[0].reshape(tok_rows, out_grad.shape[3])
    own_blocks = blocks[0]
    all_indices = lax.all_gather(pattern[0], "fsdp", axis=0, tiled=True)

    def forward_step(running, shard_blocks, first_block):
        indices = lax.dynamic_slice_in_dim(all_indices, first_block, shard_blocks.shape[0], 0)
        rows_in = jnp.take(features, indices[:, 0], axis=1)
        product = jnp.einsum(
            "tbk,bkn->tbn", rows_in, shard_blocks, preferred_element_type=jnp.float32
        )
        return running.at[:, indices[:, 1]].add(product)

    pre_zero = jnp.zeros((tok_rows, col_count, block_size), jnp.float32)
    pre_act = in_groups(
        forward_step, pre_zero, lax.all_gather(own_blocks, "fsdp", axis=0, tiled=True)
    )
    act_grad = (hidden_grad.astype(jnp.float32) * silu_slope(pre_act.reshape(tok_rows, -1))).astype(
        jnp.bfloat16
    )
    grad_cols = act_grad.reshape(tok_rows, col_count, block_size)

    def backward_step(running, shard_blocks, first_block):
        indices = lax.dynamic_slice_in_dim(all_indices, first_block, shard_blocks.shape[0], 0)
        cols_in = jnp.take(grad_cols, indices[:, 1], axis=1)
        product = jnp.einsum(
            "tbn,bkn->tbk", cols_in, shard_blocks, preferred_element_type=jnp.float32
        )
        return running.at[:, indices[:, 0]].add(product)

    back_zero = jnp.zeros((tok_rows, row_count, block_size), jnp.float32)
    input_grad = in_groups(
        backward_step, back_zero, lax.all_gather(own_blocks, "fsdp", axis=0, tiled=True)
    )
    input_grad = input_grad.astype(jnp.bfloat16).reshape(
        micro_count, activations.shape[2], activations.shape[3]
    )
    ordered = jnp.take(input_grad, order, axis=0)
    received = passed_along(ordered, "section", -1)
    indices = all_indices
    rows_in = jnp.take(features, indices[:, 0], axis=1)
    cols_in = jnp.take(grad_cols, indices[:, 1], axis=1)
    owned_grads = lax.psum_scatter(
        jnp.einsum("tbk,tbn->bkn", rows_in, cols_in, preferred_element_type=jnp.float32),
        "fsdp",
        scatter_dimension=0,
        tiled=True,
    )
    summed = lax.psum(owned_grads, "dp")
    grad_scale = 1.0 / math.sqrt(tok_rows * lax.axis_size("fsdp") * lax.axis_size("dp"))
    return (received[None], (summed * grad_scale)[None])


def solution(mesh):
    in_specs = (
        P("section", None, ("fsdp", "dp"), None),
        P("section", None, ("fsdp", "dp"), None),
        P("section", "fsdp", None, None),
        P("section", "fsdp", None),
        P(),
    )
    out_specs = (P("section", None, ("fsdp", "dp"), None), P("section", "fsdp", None, None))
    return jax.shard_map(local, mesh=mesh, in_specs=in_specs, out_specs=out_specs, check_vma=False)
```

profile of v0, /device:TPU:1, one launch (start us, length us, event | category | flops | bytes accessed | tf_op | source)
XLA Modules:
  0.0 444.8 jit_solution(14893785248069533942)
XLA Ops:
  7.2 0.0 all-gather.4.cloned.1.call-start
  7.2 0.7 all-gather.4.cloned.1.call-update
  7.9 0.0 reduce-scatter.2.cloned.1.call-start
  7.9 0.8 copy.31
  8.7 40.7 %all-gather = s32[1,128,2]{2,0,1:T(1,128)S(1)} all-gather(s32[1,4,2]{2,0,1:T(1,128)S(1)} %copy.31), channel_id=2, replica_groups=mesh['section'=2,'fsdp'=32,'dp'=4] {'fsdp'}, dimensions={1}, use_global_device_ids=true | all-gather | bytes 1056 | tf_op jit(solution)/shard_map/all_gather | solution.py:39
  49.4 0.1 copy.36
  49.5 1.6 reshape_squeeze.4
  51.1 0.4 copy.34
  51.5 5.9 %copy.41 = f32[16,8,112,128]{3,2,1,0:T(8,128)} copy(bf16[16,8,112,128]{3,1,2,0:T(8,128)(2,1)} %bitcast.51) | data formatting | bytes 11010048
  57.3 0.2 fusion.29
  57.5 3.1 gather_fusion.3
  60.6 0.2 and_reduce_fusion.1
  60.8 32.7 %all-gather.4.cloned.1.call-done = bf16[1,128,128,128]{3,2,0,1:T(8,128)(2,1)} async-done(((bf16[1,4,128,128]{3,2,0,1:T(8,128)(2,1)}), bf16[1,128,128,128]{3,2,0,1:T(8,128)(2,1)}) %all-gather.4.cloned.1.call-update) | async-done | bytes 4194320 | tf_op jit(solution)/shard_map/all_gather | solution.py:68
  93.5 3.9 broadcast_in_dim.90
  97.5 40.1 %while.26 = (s32[]{:T(128)}, f32[128,112,128]{2,0,1:T(8,128)}, s32[128,2]{0,1:T(2,128)S(1)}, bf16[128,128,128]{2,1,0:T(8,128)(2,1)}, bf16[128,28,128]{2,0,1:T(8,...) while((s32[]{:T(128)}, f32[128,112,128]{2,0,1:T(8,128)}, s32[128,2]{0,1:T(2,128)S(1)}, ...), condition=%wide.region_2.3_spmd, body=%wide.region_0.2_spmd.sunk | while | flops 135267712 | bytes 12588755 | solution.py:27
  97.5 0.1 constant_dynamic-slice_fusion.4
  97.5 1.7 gather_fusion
  99.2 2.0 fusion.43
  101.3 6.2 %scatter_fusion = f32[128,112,128]{2,0,1:T(8,128)} fusion(f32[128,112,128]{2,0,1:T(8,128)} %get-tuple-element.332, s32[32]{0:T(128)S(1)} %get-tuple-element.313, f32[32,128,128]{2,1,0:T(8,128)S(1)} %fusion.43), kind=kCustom, calls=%fused_computation.5.clone.1 | custom fusion | flops 524288 | bytes 6291584 | tf_op jit(solution)/shard_map/while/body/eval_jaxpr/scatter-add | solution.py:47
  107.5 0.1 constant_dynamic-slice_fusion.4
  107.6 1.7 gather_fusion
  109.3 2.0 fusion.43
  111.3 6.2 %scatter_fusion = f32[128,112,128]{2,0,1:T(8,128)} fusion(f32[128,112,128]{2,0,1:T(8,128)} %get-tuple-element.332, s32[32]{0:T(128)S(1)} %get-tuple-element.313, f32[32,128,128]{2,1,0:T(8,128)S(1)} %fusion.43), kind=kCustom, calls=%fused_computation.5.clone.1 | custom fusion | flops 524288 | bytes 6291584 | tf_op jit(solution)/shard_map/while/body/eval_jaxpr/scatter-add | solution.py:47
  117.5 0.1 constant_dynamic-slice_fusion.4
  117.6 1.7 gather_fusion
  119.3 2.0 fusion.43
  121.3 6.2 %scatter_fusion = f32[128,112,128]{2,0,1:T(8,128)} fusion(f32[128,112,128]{2,0,1:T(8,128)} %get-tuple-element.332, s32[32]{0:T(128)S(1)} %get-tuple-element.313, f32[32,128,128]{2,1,0:T(8,128)S(1)} %fusion.43), kind=kCustom, calls=%fused_computation.5.clone.1 | custom fusion | flops 524288 | bytes 6291584 | tf_op jit(solution)/shard_map/while/body/eval_jaxpr/scatter-add | solution.py:47
  127.5 0.1 constant_dynamic-slice_fusion.4
  127.6 1.7 gather_fusion
  129.3 2.0 fusion.43
  131.3 6.2 %scatter_fusion = f32[128,112,128]{2,0,1:T(8,128)} fusion(f32[128,112,128]{2,0,1:T(8,128)} %get-tuple-element.332, s32[32]{0:T(128)S(1)} %get-tuple-element.313, f32[32,128,128]{2,1,0:T(8,128)S(1)} %fusion.43), kind=kCustom, calls=%fused_computation.5.clone.1 | custom fusion | flops 524288 | bytes 6291584 | tf_op jit(solution)/shard_map/while/body/eval_jaxpr/scatter-add | solution.py:47
  137.5 8.5 %fusion.20 = bf16[128,112,128]{2,0,1:T(8,128)(2,1)} fusion(f32[128,112,128]{2,1,0:T(8,128)} %bitcast.49, f32[128,112,128]{2,0,1:T(8,128)} %get-tuple-element.190), kind=kLoop, calls=%fused_computation.38 | loop fusion | flops 16515072 | bytes 18350080 | tf_op jit(solution)/shard_map/convert_element_type | solution.py:53
  146.0 5.1 %gather_fusion.4 = bf16[128,128,128]{2,1,0:T(8,128)(2,1)} fusion(bf16[128,112,128]{2,0,1:T(8,128)(2,1)} %fusion.20, s32[1024]{0:T(1024)S(1)} %get-tuple-element.250), kind=kCustom, calls=%fused_computation.4 | custom fusion | bytes 8389120 | tf_op jit(solution)/shard_map/jit(_take)/gather | solution.py:77
  151.1 8.5 %fusion.21 = f32[128,128,128]{2,1,0:T(8,128)} fusion(bf16[128,128,128]{2,1,0:T(8,128)(2,1)} %gather_fusion.4, bf16[128,128,128]{2,1,0:T(8,128)(2,1)} %gather_fusion.3, pred[128]{0:T(512)(128)(4,1)S(1)} %get-tuple-element.223, pred[128]{0:T(512)(128)(4,1)S(1)} %get-tuple-element.222), kind=kOutput, calls=%fused_computation.39 | convolution fusion | flops 541065216 | bytes 16777472 | tf_op jit(solution)/shard_map/tbk,tbn->bkn/dot_general | solution.py:79
  159.7 0.2 all-reduce.2.cloned.1.call-start
  159.9 0.4 copy-done
  160.3 1.5 broadcast_in_dim.89
  161.8 45.7 %while.27 = (s32[]{:T(128)}, f32[128,28,128]{2,0,1:T(8,128)}, s32[128,2]{0,1:T(2,128)S(1)}, bf16[128,128,128]{2,1,0:T(8,128)(2,1)}, bf16[128,112,128]{2,0,1:T(8,...) while((s32[]{:T(128)}, f32[128,28,128]{2,0,1:T(8,128)}, s32[128,2]{0,1:T(2,128)S(1)}, ...), condition=%wide.region_5.6_spmd, body=%wide.region_3.5_spmd.sunk | while | flops 135267712 | bytes 12588755 | solution.py:27
  161.8 0.1 constant_dynamic-slice_fusion.5
  161.9 2.8 gather_fusion.1
  164.7 2.1 fusion.47
  166.8 6.4 %scatter_fusion.1 = f32[128,28,128]{2,0,1:T(8,128)} fusion(f32[128,28,128]{2,0,1:T(8,128)} %get-tuple-element.359, s32[32]{0:T(128)S(1)} %get-tuple-element.320, f32[32,128,128]{2,1,0:T(8,128)S(1)} %fusion.47), kind=kCustom, calls=%fused_computation.6.clone.1 | custom fusion | flops 524288 | bytes 6291584 | tf_op jit(solution)/shard_map/while/body/eval_jaxpr/scatter-add | solution.py:64
  173.2 0.1 constant_dynamic-slice_fusion.5
  173.3 2.8 gather_fusion.1
  176.1 2.1 fusion.47
  178.3 6.5 %scatter_fusion.1 = f32[128,28,128]{2,0,1:T(8,128)} fusion(f32[128,28,128]{2,0,1:T(8,128)} %get-tuple-element.359, s32[32]{0:T(128)S(1)} %get-tuple-element.320, f32[32,128,128]{2,1,0:T(8,128)S(1)} %fusion.47), kind=kCustom, calls=%fused_computation.6.clone.1 | custom fusion | flops 524288 | bytes 6291584 | tf_op jit(solution)/shard_map/while/body/eval_jaxpr/scatter-add | solution.py:64
  184.7 0.1 constant_dynamic-slice_fusion.5
  184.8 2.8 gather_fusion.1
  187.6 2.1 fusion.47
  189.8 6.3 %scatter_fusion.1 = f32[128,28,128]{2,0,1:T(8,128)} fusion(f32[128,28,128]{2,0,1:T(8,128)} %get-tuple-element.359, s32[32]{0:T(128)S(1)} %get-tuple-element.320, f32[32,128,128]{2,1,0:T(8,128)S(1)} %fusion.47), kind=kCustom, calls=%fused_computation.6.clone.1 | custom fusion | flops 524288 | bytes 6291584 | tf_op jit(solution)/shard_map/while/body/eval_jaxpr/scatter-add | solution.py:64
  196.1 0.1 constant_dynamic-slice_fusion.5
  196.1 2.9 gather_fusion.1
  199.1 2.1 fusion.47
  201.2 6.3 %scatter_fusion.1 = f32[128,28,128]{2,0,1:T(8,128)} fusion(f32[128,28,128]{2,0,1:T(8,128)} %get-tuple-element.359, s32[32]{0:T(128)S(1)} %get-tuple-element.320, f32[32,128,128]{2,1,0:T(8,128)S(1)} %fusion.47), kind=kCustom, calls=%fused_computation.6.clone.1 | custom fusion | flops 524288 | bytes 6291584 | tf_op jit(solution)/shard_map/while/body/eval_jaxpr/scatter-add | solution.py:64
  207.5 1.6 convert_element_type.17
  209.1 0.6 copy.37
  209.8 0.5 reshape.37
  210.3 0.6 gather_fusion.2
  210.9 0.2 broadcast_select_fusion
  211.0 1.3 collective-permute-start
  212.3 172.1 %reduce-scatter.2.cloned.1.call-done = f32[4,128,128]{2,1,0:T(8,128)} async-done(((f32[128,128,128]{2,1,0:T(8,128)}), f32[4,128,128]{2,1,0:T(8,128)}) %reduce-scatter.2.cloned.1.call-update) | async-done | bytes 262160 | tf_op jit(solution)/shard_map/reduce_scatter | solution.py:78
  384.5 51.2 %all-reduce.2.cloned.1.call-done = f32[4,128,128]{2,1,0:T(8,128)} async-done(((f32[4,128,128]{2,1,0:T(8,128)}), f32[4,128,128]{2,1,0:T(8,128)}) %all-reduce.2.cloned.1.call-update) | async-done | bytes 262160 | tf_op jit(solution)/shard_map/psum | solution.py:84
  435.7 1.7 multiply_bitcast_fusion
  437.3 0.9 copy.61
  (32 shorter events, 0.3 us)
Async XLA Ops:
  7.2 86.3 %all-gather.4.cloned.1.call-start = ((), (), s32[]{:S(2)}) async-start(), calls=%async_computation.3 | async-start | bytes 4325376 | tf_op jit(solution)/shard_map/all_gather | solution.py:68
  7.9 376.5 %reduce-scatter.2.cloned.1.call-start = ((), (), s32[]{:S(2)}) async-start(), calls=%async_computation.1 | async-start | bytes 8650752 | tf_op jit(solution)/shard_map/reduce_scatter | solution.py:78
  159.6 0.7 copy-start
  159.7 276.0 %all-reduce.2.cloned.1.call-start = ((), (), s32[]{:S(2)}) async-start(), calls=%async_computation.2 | async-start | bytes 524288 | tf_op jit(solution)/shard_map/psum | solution.py:84
  211.0 173.4 %collective-permute-start = (bf16[4,32,3584]{2,1,0:T(8,128)(2,1)S(1)}, bf16[4,32,3584]{2,1,0:T(8,128)(2,1)S(1)}, u32[]{:S(2)}, u32[]{:S(2)}) collective-permute-start(bf16[4,32,3584]{2,1,0:T(8,128)(2,1)S(1)} %broadcast_select_fusion), channel_id=1, source_target_pairs={{128,0},{129,1},{130,2},{131,3},{132,4},{133,5},{134,6},{135,7},{1... | collective-permute-start | bytes 2752520 | tf_op jit(solution)/shard_map/ppermute | solution.py:11
Sparse Core Ops, SparseCore 0:
  10.6 82.8 all-gather.3
  159.8 224.6 reduce-scatter.1
  387.3 48.3 all-reduce.1
where the time goes:
time: 447 us; the launch traced here: 445 us
  waiting for transfers between devices  257 us (57%)
  other arithmetic  62.9 us (14%)
  local copies, waits for them, and re-layouts  43.9 us (10%)
  blocking collectives  40.7 us (9%)
  matrix products  25.1 us (6%)
  between operations  13.8 us (3%)
    reduce_scatter x1, waiting for transfers between devices, local(): lax.psum_scatter(jnp.einsum('tbk,tbn->bkn', rows_in, cols_in, preferred_e...  172 us
    psum x1, waiting for transfers between devices, local(): summed = lax.psum(owned_grads, 'dp')  51.2 us
    all_gather x1, blocking collectives, local(): all_indices = lax.all_gather(pattern[0], 'fsdp', axis=0, tiled=True)  40.7 us
    all_gather x1, waiting for transfers between devices, local(): lax.all_gather(own_blocks, 'fsdp', axis=0, tiled=True)  32.7 us
    scatter-add x4, other arithmetic, backward_step(): return running.at[:, indices[:, 0]].add(product)  25.5 us
    scatter-add x4, other arithmetic, forward_step(): return running.at[:, indices[:, 1]].add(product)  24.8 us
    gather x4, local copies, waits for them, and re-layouts, backward_step(): cols_in = jnp.take(grad_cols, indices[:, 1], axis=1)  11.3 us
  transfers between devices with their start and end apart: 4, of which 3 were waited for; matrix products, arithmetic and copies ran while one was open for 14% of the time, Pallas kernels for 0%

commit v1 on v0

--- a/solution.py
+++ b/solution.py
@@ -3,6 +3,7 @@
 import jax.numpy as jnp
 from jax import lax
 from jax.sharding import PartitionSpec as P
+from jax.lax import all_gather
 
 
 def passed_along(block, axis, distance):
@@ -81,7 +82,7 @@
         scatter_dimension=0,
         tiled=True,
     )
-    summed = lax.psum(owned_grads, "dp")
+    summed = jnp.sum(all_gather(owned_grads, "dp"), axis=0)
     grad_scale = 1.0 / math.sqrt(tok_rows * lax.axis_size("fsdp") * lax.axis_size("dp"))
     return (received[None], (summed * grad_scale)[None])
 

time: 447 us -> 425 us (0.951)
  waiting for transfers between devices: 257 us -> 233 us
    psum x1 -> x0, waiting for transfers between devices: 51.2 us -> none  [local(): summed = lax.psum(owned_grads, 'dp')]
    ppermute x1, waiting for transfers between devices: 0.01 us -> 17.8 us  [passed_along(): return lax.ppermute(block, axis, route)]
    all_gather x0 -> x1, waiting for transfers between devices: none -> 8.71 us  [local(): summed = jnp.sum(all_gather(owned_grads, 'dp'), axis=0)]
  transfers between devices with their start and end apart: 4 -> 4, of which waited for: 3 -> 4; matrix products, arithmetic and copies ran while one was open for 14% -> 15% of each run, Pallas kernels for 0% -> 0%
where the time goes in v1:
time: 425 us; the launch traced here: 422 us
  waiting for transfers between devices  233 us (55%)
  other arithmetic  63.2 us (15%)
  local copies, waits for them, and re-layouts  43.9 us (10%)
  blocking collectives  40.7 us (10%)
  matrix products  25.1 us (6%)
  between operations  13.8 us (3%)
    reduce_scatter x1, waiting for transfers between devices, local(): lax.psum_scatter(jnp.einsum('tbk,tbn->bkn', rows_in, cols_in, preferred_e...  174 us
    all_gather x1, blocking collectives, local(): all_indices = lax.all_gather(pattern[0], 'fsdp', axis=0, tiled=True)  40.7 us
    all_gather x1, waiting for transfers between devices, local(): lax.all_gather(own_blocks, 'fsdp', axis=0, tiled=True)  32.7 us
    scatter-add x4, other arithmetic, backward_step(): return running.at[:, indices[:, 0]].add(product)  25.5 us
    scatter-add x4, other arithmetic, forward_step(): return running.at[:, indices[:, 1]].add(product)  24.8 us
    ppermute x1, waiting for transfers between devices, passed_along(): return lax.ppermute(block, axis, route)  17.8 us
    gather x4, local copies, waits for them, and re-layouts, backward_step(): cols_in = jnp.take(grad_cols, indices[:, 1], axis=1)  11.3 us
    all_gather x1, waiting for transfers between devices, local(): summed = jnp.sum(all_gather(owned_grads, 'dp'), axis=0)  8.71 us
  transfers between devices with their start and end apart: 4, of which 4 were waited for; matrix products, arithmetic and copies ran while one was open for 15% of the time, Pallas kernels for 0%

profile of v1, /device:TPU:1, one launch (start us, length us, event | category | flops | bytes accessed | tf_op | source)
XLA Modules:
  0.0 421.9 jit_solution(7748221262667150776)
XLA Ops:
  7.2 0.7 all-gather.6.cloned.1.call-update
  7.9 0.8 copy.31
  8.7 40.7 %all-gather = s32[1,128,2]{2,0,1:T(1,128)S(1)} all-gather(s32[1,4,2]{2,0,1:T(1,128)S(1)} %copy.31), channel_id=2, replica_groups=mesh['section'=2,'fsdp'=32,'dp'=4] {'fsdp'}, dimensions={1}, use_global_device_ids=true | all-gather | bytes 1056 | tf_op jit(solution)/shard_map/all_gather | solution.py:40
  49.4 0.1 copy.36
  49.5 1.6 reshape_squeeze.4
  51.1 0.4 copy.34
  51.5 5.9 %copy.41 = f32[16,8,112,128]{3,2,1,0:T(8,128)} copy(bf16[16,8,112,128]{3,1,2,0:T(8,128)(2,1)} %bitcast.52) | data formatting | bytes 11010048
  57.3 0.2 fusion.29
  57.5 3.1 gather_fusion.3
  60.6 0.2 and_reduce_fusion.1
  60.8 32.7 %all-gather.6.cloned.1.call-done = bf16[1,128,128,128]{3,2,0,1:T(8,128)(2,1)} async-done(((bf16[1,4,128,128]{3,2,0,1:T(8,128)(2,1)}), bf16[1,128,128,128]{3,2,0,1:T(8,128)(2,1)}) %all-gather.6.cloned.1.call-update) | async-done | bytes 4194320 | tf_op jit(solution)/shard_map/all_gather | solution.py:69
  93.5 3.9 broadcast_in_dim.88
  97.5 40.1 %while.26 = (s32[]{:T(128)}, f32[128,112,128]{2,0,1:T(8,128)}, s32[128,2]{0,1:T(2,128)S(1)}, bf16[128,128,128]{2,1,0:T(8,128)(2,1)}, bf16[128,28,128]{2,0,1:T(8,...) while((s32[]{:T(128)}, f32[128,112,128]{2,0,1:T(8,128)}, s32[128,2]{0,1:T(2,128)S(1)}, ...), condition=%wide.region_2.3_spmd, body=%wide.region_0.2_spmd.sunk | while | flops 135267712 | bytes 12588755 | solution.py:28
  97.5 0.1 constant_dynamic-slice_fusion.4
  97.5 1.7 gather_fusion
  99.2 2.0 fusion.43
  101.3 6.2 %scatter_fusion = f32[128,112,128]{2,0,1:T(8,128)} fusion(f32[128,112,128]{2,0,1:T(8,128)} %get-tuple-element.332, s32[32]{0:T(128)S(1)} %get-tuple-element.313, f32[32,128,128]{2,1,0:T(8,128)S(1)} %fusion.43), kind=kCustom, calls=%fused_computation.5.clone.1 | custom fusion | flops 524288 | bytes 6291584 | tf_op jit(solution)/shard_map/while/body/eval_jaxpr/scatter-add | solution.py:48
  107.5 0.1 constant_dynamic-slice_fusion.4
  107.6 1.7 gather_fusion
  109.3 2.0 fusion.43
  111.3 6.2 %scatter_fusion = f32[128,112,128]{2,0,1:T(8,128)} fusion(f32[128,112,128]{2,0,1:T(8,128)} %get-tuple-element.332, s32[32]{0:T(128)S(1)} %get-tuple-element.313, f32[32,128,128]{2,1,0:T(8,128)S(1)} %fusion.43), kind=kCustom, calls=%fused_computation.5.clone.1 | custom fusion | flops 524288 | bytes 6291584 | tf_op jit(solution)/shard_map/while/body/eval_jaxpr/scatter-add | solution.py:48
  117.5 0.1 constant_dynamic-slice_fusion.4
  117.6 1.7 gather_fusion
  119.3 2.0 fusion.43
  121.3 6.2 %scatter_fusion = f32[128,112,128]{2,0,1:T(8,128)} fusion(f32[128,112,128]{2,0,1:T(8,128)} %get-tuple-element.332, s32[32]{0:T(128)S(1)} %get-tuple-element.313, f32[32,128,128]{2,1,0:T(8,128)S(1)} %fusion.43), kind=kCustom, calls=%fused_computation.5.clone.1 | custom fusion | flops 524288 | bytes 6291584 | tf_op jit(solution)/shard_map/while/body/eval_jaxpr/scatter-add | solution.py:48
  127.5 0.1 constant_dynamic-slice_fusion.4
  127.6 1.7 gather_fusion
  129.3 2.0 fusion.43
  131.3 6.2 %scatter_fusion = f32[128,112,128]{2,0,1:T(8,128)} fusion(f32[128,112,128]{2,0,1:T(8,128)} %get-tuple-element.332, s32[32]{0:T(128)S(1)} %get-tuple-element.313, f32[32,128,128]{2,1,0:T(8,128)S(1)} %fusion.43), kind=kCustom, calls=%fused_computation.5.clone.1 | custom fusion | flops 524288 | bytes 6291584 | tf_op jit(solution)/shard_map/while/body/eval_jaxpr/scatter-add | solution.py:48
  137.5 8.5 %fusion.20 = bf16[128,112,128]{2,0,1:T(8,128)(2,1)} fusion(f32[128,112,128]{2,1,0:T(8,128)} %bitcast.50, f32[128,112,128]{2,0,1:T(8,128)} %get-tuple-element.190), kind=kLoop, calls=%fused_computation.38 | loop fusion | flops 16515072 | bytes 18350080 | tf_op jit(solution)/shard_map/convert_element_type | solution.py:54
  146.0 5.1 %gather_fusion.4 = bf16[128,128,128]{2,1,0:T(8,128)(2,1)} fusion(bf16[128,112,128]{2,0,1:T(8,128)(2,1)} %fusion.20, s32[1024]{0:T(1024)S(1)} %get-tuple-element.250), kind=kCustom, calls=%fused_computation.4 | custom fusion | bytes 8389120 | tf_op jit(solution)/shard_map/jit(_take)/gather | solution.py:78
  151.1 8.5 %fusion.21 = f32[128,128,128]{2,1,0:T(8,128)} fusion(bf16[128,128,128]{2,1,0:T(8,128)(2,1)} %gather_fusion.4, bf16[128,128,128]{2,1,0:T(8,128)(2,1)} %gather_fusion.3, pred[128]{0:T(512)(128)(4,1)S(1)} %get-tuple-element.223, pred[128]{0:T(512)(128)(4,1)S(1)} %get-tuple-element.222), kind=kOutput, calls=%fused_computation.39 | convolution fusion | flops 541065216 | bytes 16777472 | tf_op jit(solution)/shard_map/tbk,tbn->bkn/dot_general | solution.py:80
  159.7 0.2 all-gather.8.cloned.1.call-start
  159.9 0.4 copy-done
  160.3 1.5 broadcast_in_dim.87
  161.8 45.7 %while.27 = (s32[]{:T(128)}, f32[128,28,128]{2,0,1:T(8,128)}, s32[128,2]{0,1:T(2,128)S(1)}, bf16[128,128,128]{2,1,0:T(8,128)(2,1)}, bf16[128,112,128]{2,0,1:T(8,...) while((s32[]{:T(128)}, f32[128,28,128]{2,0,1:T(8,128)}, s32[128,2]{0,1:T(2,128)S(1)}, ...), condition=%wide.region_5.6_spmd, body=%wide.region_3.5_spmd.sunk | while | flops 135267712 | bytes 12588755 | solution.py:28
  161.8 0.1 constant_dynamic-slice_fusion.5
  161.9 2.8 gather_fusion.1
  164.7 2.1 fusion.47
  166.8 6.4 %scatter_fusion.1 = f32[128,28,128]{2,0,1:T(8,128)} fusion(f32[128,28,128]{2,0,1:T(8,128)} %get-tuple-element.359, s32[32]{0:T(128)S(1)} %get-tuple-element.320, f32[32,128,128]{2,1,0:T(8,128)S(1)} %fusion.47), kind=kCustom, calls=%fused_computation.6.clone.1 | custom fusion | flops 524288 | bytes 6291584 | tf_op jit(solution)/shard_map/while/body/eval_jaxpr/scatter-add | solution.py:65
  173.2 0.1 constant_dynamic-slice_fusion.5
  173.3 2.8 gather_fusion.1
  176.1 2.1 fusion.47
  178.3 6.5 %scatter_fusion.1 = f32[128,28,128]{2,0,1:T(8,128)} fusion(f32[128,28,128]{2,0,1:T(8,128)} %get-tuple-element.359, s32[32]{0:T(128)S(1)} %get-tuple-element.320, f32[32,128,128]{2,1,0:T(8,128)S(1)} %fusion.47), kind=kCustom, calls=%fused_computation.6.clone.1 | custom fusion | flops 524288 | bytes 6291584 | tf_op jit(solution)/shard_map/while/body/eval_jaxpr/scatter-add | solution.py:65
  184.7 0.1 constant_dynamic-slice_fusion.5
  184.8 2.8 gather_fusion.1
  187.6 2.1 fusion.47
  189.8 6.3 %scatter_fusion.1 = f32[128,28,128]{2,0,1:T(8,128)} fusion(f32[128,28,128]{2,0,1:T(8,128)} %get-tuple-element.359, s32[32]{0:T(128)S(1)} %get-tuple-element.320, f32[32,128,128]{2,1,0:T(8,128)S(1)} %fusion.47), kind=kCustom, calls=%fused_computation.6.clone.1 | custom fusion | flops 524288 | bytes 6291584 | tf_op jit(solution)/shard_map/while/body/eval_jaxpr/scatter-add | solution.py:65
  196.1 0.1 constant_dynamic-slice_fusion.5
  196.1 2.9 gather_fusion.1
  199.1 2.1 fusion.47
  201.2 6.3 %scatter_fusion.1 = f32[128,28,128]{2,0,1:T(8,128)} fusion(f32[128,28,128]{2,0,1:T(8,128)} %get-tuple-element.359, s32[32]{0:T(128)S(1)} %get-tuple-element.320, f32[32,128,128]{2,1,0:T(8,128)S(1)} %fusion.47), kind=kCustom, calls=%fused_computation.6.clone.1 | custom fusion | flops 524288 | bytes 6291584 | tf_op jit(solution)/shard_map/while/body/eval_jaxpr/scatter-add | solution.py:65
  207.5 1.6 convert_element_type.17
  209.1 0.6 copy.37
  209.8 0.5 reshape.46
  210.3 0.6 gather_fusion.2
  210.9 173.5 %reduce-scatter.2.cloned.1.call-done = f32[4,128,128]{2,1,0:T(8,128)} async-done(((f32[128,128,128]{2,1,0:T(8,128)}), f32[4,128,128]{2,1,0:T(8,128)}) %reduce-scatter.2.cloned.1.call-update) | async-done | bytes 262160 | tf_op jit(solution)/shard_map/reduce_scatter | solution.py:79
  384.4 0.2 broadcast_select_fusion
  384.6 1.3 collective-permute-start
  385.9 17.8 %collective-permute-done = bf16[4,32,3584]{2,1,0:T(8,128)(2,1)S(1)} collective-permute-done((bf16[4,32,3584]{2,1,0:T(8,128)(2,1)S(1)}, bf16[4,32,3584]{2,1,0:T(8,128)(2,1)S(1)}, u32[]{:S(2)}, u32[]{:S(2)}) %collective-permute-start) | collective-permute-done | bytes 917536 | tf_op jit(solution)/shard_map/ppermute | solution.py:12
  403.7 8.7 %all-gather.8.cloned.1.call-done = f32[16,128,128]{2,1,0:T(8,128)} async-done(((f32[4,128,128]{2,1,0:T(8,128)}), f32[16,128,128]{2,1,0:T(8,128)}) %all-gather.8.cloned.1.call-update) | async-done | bytes 1048592 | tf_op jit(solution)/shard_map/all_gather | solution.py:85
  412.4 1.3 reduce_sum.9
  413.7 0.7 multiply_bitcast_fusion
  414.5 0.9 copy.60
  (33 shorter events, 0.3 us)
Async XLA Ops:
  7.2 86.3 %all-gather.6.cloned.1.call-start = ((), (), s32[]{:S(2)}) async-start(), calls=%async_computation.2 | async-start | bytes 4325376 | tf_op jit(solution)/shard_map/all_gather | solution.py:69
  7.9 376.5 %reduce-scatter.2.cloned.1.call-start = ((), (), s32[]{:S(2)}) async-start(), calls=%async_computation.1 | async-start | bytes 8650752 | tf_op jit(solution)/shard_map/reduce_scatter | solution.py:79
  159.6 0.7 copy-start
  159.7 252.8 %all-gather.8.cloned.1.call-start = ((), (), s32[]{:S(2)}) async-start(), calls=%async_computation.3 | async-start | bytes 1310720 | tf_op jit(solution)/shard_map/all_gather | solution.py:85
  384.6 19.1 %collective-permute-start = (bf16[4,32,3584]{2,1,0:T(8,128)(2,1)S(1)}, bf16[4,32,3584]{2,1,0:T(8,128)(2,1)S(1)}, u32[]{:S(2)}, u32[]{:S(2)}) collective-permute-start(bf16[4,32,3584]{2,1,0:T(8,128)(2,1)S(1)} %broadcast_select_fusion), channel_id=1, source_target_pairs={{128,0},{129,1},{130,2},{131,3},{132,4},{133,5},{134,6},{135,7},{1... | collective-permute-start | bytes 2752520 | tf_op jit(solution)/shard_map/ppermute | solution.py:12
Sparse Core Ops, SparseCore 0:
  10.6 82.8 all-gather.5
  159.8 224.5 reduce-scatter.1
  386.4 26.0 all-gather.7
